TPU v7x, 32 devices: a whole 2x2x4 slice. The times are simulated.
32 devices in a mesh: feed: 4 (over y, x), freq: 8 (over z, core).
Axes of the slice: x: 2, y: 2, z: 4, core: 2. Of those that a mesh axis runs over, the one named last changes fastest.
Arguments:
- voltage: bfloat16 [2, 1024, 32768], P(None, 'feed', 'freq'), may hold values from -6 to 6
- flags: int32 [4, 128], P('feed'), may hold values 0 or 1
- owner_slot: int32 [128], replicated, may hold values from 0 to 159, as said below
Outputs:
- visibility: bfloat16 [160, 2, 1024, 1024], P('freq', None, 'feed')
Inputs may be any that keep to these rules, and one draw needn't show every extreme that they name: `owner_slot`: distinct slots; slot s belongs to owner s // 20 of freq. No owner gets more than 20 channels, and some owner gets exactly 20.
All inputs are finite; a program needn't handle non-finite values. No bound on the sum of `flags` on one device may be relied on, other than what follows from the above.
Results may differ from a plain program's by a relative error of at most 0.0073.
Values may be sent and summed in bfloat16 or wider, within the bound.
A program may use at most 192 MiB of HBM per device.

v0:
```python
import math

import jax
import jax.numpy as jnp
from jax import lax
from jax.sharding import PartitionSpec as P

CH = 1024
TAPS = 4
BAND_LO = 256
CAP = 20


def passed_along(value, axis, steps):
    count = lax.axis_size(axis)
    initial, last = (max(0, -steps), min(count, count - steps))
    return lax.ppermute(value, axis, [(source, source + steps) for source in range(initial, last)])


def prototype():
    total = TAPS * CH
    position = jnp.arange(total, dtype=jnp.int32).astype(jnp.float32)
    offset = (position - total / 2 + 0.5) / CH
    taper = 0.5 - 0.5 * jnp.cos(2 * jnp.pi * (position + 0.5) / total)
    coeffs = jnp.sinc(offset) * taper
    coeffs = coeffs * jnp.sqrt(CH / jnp.sum(coeffs * coeffs))
    return coeffs.reshape(TAPS, CH)


def tables(band):
    sample = jnp.arange(CH, dtype=jnp.int32)
    channel = jnp.arange(band, dtype=jnp.int32) + BAND_LO
    phase = (sample[:, None] * channel[None, :] % CH).astype(jnp.float32) * (2 * jnp.pi / CH)
    return (jnp.cos(phase).astype(jnp.bfloat16), jnp.sin(phase).astype(jnp.bfloat16))


def channelize(voltage, extra, flag_row):
    band = flag_row.shape[0]
    longer = jnp.concatenate([voltage, extra], 2)
    count = voltage.shape[2] // CH
    feeds = voltage.shape[1]
    blocks = longer.reshape(2, feeds, count + TAPS - 1, CH)
    coeffs = prototype()
    summed = blocks[:, :, 0:count, :].astype(jnp.float32) * coeffs[0]
    for tap_index in range(1, TAPS):
        summed = (
            summed
            + blocks[:, :, tap_index : tap_index + count, :].astype(jnp.float32) * coeffs[tap_index]
        )
    weighted = summed.astype(jnp.bfloat16)
    cosine, sine = tables(band)
    real_rows = weighted[0].reshape(feeds * count, CH)
    imag_rows = weighted[1].reshape(feeds * count, CH)
    real_part = jnp.dot(real_rows, cosine, preferred_element_type=jnp.float32) + jnp.dot(
        imag_rows, sine, preferred_element_type=jnp.float32
    )
    imag_part = jnp.dot(imag_rows, cosine, preferred_element_type=jnp.float32) - jnp.dot(
        real_rows, sine, preferred_element_type=jnp.float32
    )
    joined = jnp.stack([real_part, imag_part], 0).reshape(2, feeds, count, band)
    joined = joined * (flag_row.astype(jnp.float32) * (1.0 / math.sqrt(CH)))
    return jnp.transpose(joined, (3, 0, 2, 1)).astype(jnp.bfloat16)


def correlate(own_rows, columns, inverse):
    swapped = jnp.stack([columns[:, :, 1], -columns[:, :, 0]], 2)
    real_vis = jnp.einsum("cpzsf,cpzsg->cfg", own_rows, columns, preferred_element_type=jnp.float32)
    imag_vis = jnp.einsum("cpzsf,cpzsg->cfg", own_rows, swapped, preferred_element_type=jnp.float32)
    return (jnp.stack([real_vis, imag_vis], 1) * inverse).astype(jnp.bfloat16)


def body(voltage, flags, owner_slot):
    tail_width = (TAPS - 1) * CH
    incoming = passed_along(voltage[:, :, :tail_width], "freq", -1)
    spectra = channelize(voltage, incoming, flags[0])
    owners = lax.axis_size("freq")
    band = owner_slot.shape[0]
    row_index = jnp.arange(CAP * owners, dtype=jnp.int32)
    slot_ids = row_index % owners * CAP + row_index // owners
    selector = (owner_slot[None, :] == slot_ids[:, None]).astype(jnp.bfloat16)
    inverse = 1.0 / (owners * spectra.shape[2])
    complete = lax.all_gather(spectra, "feed", axis=3, tiled=True)
    flat = complete.reshape(band, -1)
    placed = jnp.dot(selector, flat, preferred_element_type=jnp.float32).astype(jnp.bfloat16)
    received = lax.all_to_all(
        placed.reshape((CAP, owners) + complete.shape[1:]),
        "freq",
        split_axis=1,
        concat_axis=1,
        tiled=True,
    )
    width = spectra.shape[3]
    own_rows = lax.dynamic_slice_in_dim(received, lax.axis_index("feed") * width, width, 4)
    result = correlate(own_rows, received, inverse)
    return result


def solution(mesh):
    placed = (P(None, "feed", "freq"), P("feed", None), P())
    return jax.shard_map(
        body, mesh=mesh, in_specs=placed, out_specs=P("freq", None, "feed", None), check_vma=False
    )
```

profile of v0, /device:TPU:0, one launch (start us, length us, event | category | flops | bytes accessed | tf_op | source)
XLA Modules:
  0.0 255.4 jit_solution(4901334823485073540)
XLA Ops:
  6.5 0.0 all-gather.2.cloned.1.call-start
  6.5 6.3 %copy.21 = bf16[2,256,4096]{1,2,0:T(8,128)(2,1)} copy(bf16[2,256,4096]{2,1,0:T(8,128)(2,1)} %param.3) | data formatting | bytes 8388608 | tf_op args[0]
  12.9 0.0 copy-start.3
  12.9 3.8 %slice.56 = bf16[2,256,3072]{1,2,0:T(8,128)(2,1)} slice(bf16[2,256,4096]{1,2,0:T(8,128)(2,1)} %copy.21), slice={[0:2], [0:256], [0:3072]} | slice | bytes 6291456 | tf_op jit(solution)/shard_map/slice | solution.py:74
  16.6 1.3 collective-permute-start
  17.9 0.8 multiply_reduce_fusion
  19.4 0.1 broadcast_multiply_fusion
  19.5 0.0 copy-done.3
  19.6 4.8 %collective-permute-done = bf16[2,256,3072]{1,2,0:T(8,128)(2,1)S(1)} collective-permute-done((bf16[2,256,3072]{1,2,0:T(8,128)(2,1)}, bf16[2,256,3072]{1,2,0:T(8,128)(2,1)S(1)}, u32[]{:S(2)}, u32[]{:S(2)}) %collective-permute-start) | collective-permute-done | bytes 3145760 | tf_op jit(solution)/shard_map/ppermute | solution.py:17
  24.4 5.7 %pad_maximum_fusion = bf16[2,256,7168]{1,2,0:T(8,128)(2,1)} fusion(bf16[2,256,3072]{1,2,0:T(8,128)(2,1)S(1)} %collective-permute-done, bf16[2,256,4096]{1,2,0:T(8,128)(2,1)} %copy.21), kind=kLoop, calls=%fused_computation.6 | loop fusion | flops 14680064 | bytes 14680064 | tf_op jit(solution)/shard_map/concatenate | solution.py:39
  30.1 9.2 %add_convert_fusion = bf16[2,256,4,1024]{1,3,2,0:T(8,128)(2,1)S(1)} fusion(bf16[2,256,7,1024]{1,3,2,0:T(8,128)(2,1)} %bitcast.27, f32[1024]{0:T(1024)S(1)} %get-tuple-element.10, f32[1024]{0:T(1024)S(1)} %get-tuple-element.11, f32[1024]{0:T(1024)S(1)} %get-tuple-element.12, f32[1024]{0:T(1024)S(1)} %get-tuple-element.9), kind=kLoop, calls=%fused_computation.5 | loop fusion | flops 25165824 | bytes 20987904 | tf_op jit(solution)/shard_map/convert_element_type | solution.py:50
  39.3 2.3 fusion.55
  41.6 3.4 %copy.22 = bf16[1,256,4,1024]{3,2,1,0:T(4,128)(2,1)S(1)} copy(bf16[1,256,4,1024]{1,3,2,0:T(8,128)(2,1)} %get-tuple-element.5) | data formatting | bytes 4194304 | tf_op jit(solution)/shard_map/slice | solution.py:52
  44.9 2.1 reshape_squeeze.6
  47.0 3.4 %copy.23 = bf16[1,256,4,1024]{3,2,1,0:T(4,128)(2,1)S(1)} copy(bf16[1,256,4,1024]{1,3,2,0:T(8,128)(2,1)} %get-tuple-element.6) | data formatting | bytes 4194304 | tf_op jit(solution)/shard_map/slice | solution.py:53
  50.4 2.0 reshape_squeeze.7
  52.4 0.0 copy-start.1
  52.4 4.1 %fusion.15 = f32[1024,128]{1,0:T(8,128)S(1)} fusion(bf16[1024,1024]{1,0:T(8,128)(2,1)} %reshape_squeeze.6, s32[128]{0:T(128)S(1)} %iota_add_fusion), kind=kOutput, calls=%fused_computation.30 | convolution fusion | flops 270401536 | bytes 2621952 | tf_op jit(solution)/shard_map/dot_general | solution.py:54
  56.5 0.0 copy-done.1
  56.5 2.4 fusion.14
  58.9 0.0 copy-start
  58.9 2.4 convolution_add_fusion
  61.3 0.0 copy-done
  61.3 2.4 convolution_subtract_fusion
  63.8 0.0 copy-start.2
  63.9 0.9 fusion.10
  64.7 0.0 all-gather.2.cloned.1.call-update
  64.8 67.8 %all-gather.2.cloned.1.call-done = bf16[128,2,4,1024]{0,3,2,1:T(8,128)(2,1)} async-done(((bf16[128,2,4,256]{0,3,2,1:T(8,128)(2,1)}), bf16[128,2,4,1024]{0,3,2,1:T(8,128)(2,1)}) %all-gather.2.cloned.1.call-update) | async-done | bytes 2097168 | tf_op jit(solution)/shard_map/all_gather | solution.py:82
  132.6 0.0 copy-done.2
  132.6 2.5 convolution_convert_fusion
  135.0 4.4 %copy.26 = bf16[20,8,2,4,1024]{4,2,0,3,1:T(2,128)(2,1)} copy(bf16[20,8,2,4,1024]{4,1,3,2,0:T(8,128)(2,1)S(1)} %bitcast.28) | data formatting | bytes 5242880 | tf_op jit(solution)/shard_map/reshape | solution.py:86
  139.5 4.6 %all-to-all-start = ((bf16[20,8,2,4,1024]{4,2,0,3,1:T(2,128)(2,1)}), bf16[20,8,2,4,1024]{4,2,0,3,1:T(2,128)(2,1)S(1)}, u32[]{:S(2)}, u32[]{:S(2)}) async-start(bf16[20,8,2,4,1024]{4,2,0,3,1:T(2,128)(2,1)} %copy.26), calls=%async_computation | async-start | bytes 5242880 | tf_op jit(solution)/shard_map/all_to_all | solution.py:85
  144.1 60.3 %all-to-all-done = bf16[20,8,2,4,1024]{4,2,0,3,1:T(2,128)(2,1)S(1)} async-done(((bf16[20,8,2,4,1024]{4,2,0,3,1:T(2,128)(2,1)}), bf16[20,8,2,4,1024]{4,2,0,3,1:T(2,128)(2,1)S(1)}, u32[]{:S(2)}, u32[]{:S(2)}) %all-to-all-start) | async-done | bytes 2621472 | tf_op jit(solution)/shard_map/all_to_all | solution.py:85
  204.4 2.8 %copy.27 = bf16[20,8,2,4,1024]{4,1,2,0,3:T(8,128)(2,1)S(1)} copy(bf16[20,8,2,4,1024]{4,2,0,3,1:T(2,128)(2,1)S(1)} %all-to-all-done) | data formatting | bytes 5242880 | tf_op jit(solution)/shard_map/all_to_all | solution.py:85
  207.2 0.2 fusion.56
  207.3 8.5 %convolution_bitcast_fusion.1 = f32[20,1,256,1024]{3,2,0,1:T(8,128)} fusion(bf16[20,8,2,4,1024]{4,1,2,0,3:T(8,128)(2,1)S(1)} %copy.27, s32[]{:T(128)S(6)} %select_n.75), kind=kOutput, calls=%fused_computation.4 | convolution fusion | flops 671088640 | bytes 24248324 | tf_op jit(solution)/shard_map/cpzsf,cpzsg->cfg/dot_general | solution.py:67
  215.9 9.1 %convolution_bitcast_fusion = f32[20,1,256,1024]{3,2,0,1:T(8,128)} fusion(bf16[20,8,1,4,1024]{4,1,2,0,3:T(8,128)(2,1)S(1)} %get-tuple-element.8, bf16[20,8,1,4,1024]{4,1,2,0,3:T(8,128)(2,1)S(1)} %get-tuple-element.7, bf16[20,8,2,4,1024]{4,1,2,0,3:T(8,128)(2,1)S(1)} %copy.27, s32[]{:T(128)S(6)} %select_n.75), kind=kOutput, calls=%fused_computation.3 | convolution fusion | flops 672399360 | bytes 24248324 | tf_op jit(solution)/shard_map/cpzsf,cpzsg->cfg/dot_general | solution.py:68
  225.0 16.2 %fusion = bf16[20,2,256,1024]{3,2,0,1:T(8,128)(2,1)S(1)} fusion(f32[20,1,256,1024]{3,2,0,1:T(8,128)} %convolution_bitcast_fusion, f32[20,1,256,1024]{3,2,0,1:T(8,128)} %convolution_bitcast_fusion.1), kind=kLoop, calls=%fused_computation.1 | loop fusion | flops 31457280 | bytes 62914560 | tf_op jit(solution)/shard_map/convert_element_type | solution.py:69
  241.2 7.3 %copy.31 = bf16[20,2,256,1024]{3,2,1,0:T(8,128)(2,1)} copy(bf16[20,2,256,1024]{3,2,0,1:T(8,128)(2,1)S(1)} %fusion) | data formatting | bytes 41943040 | tf_op jit(solution)/shard_map/convert_element_type | solution.py:69
  (6 shorter events, 0.1 us)
Async XLA Ops:
  6.5 126.0 %all-gather.2.cloned.1.call-start = ((), (), s32[]{:S(2)}) async-start(), calls=%async_computation.1 | async-start | bytes 2621440 | tf_op jit(solution)/shard_map/all_gather | solution.py:82
  12.9 6.7 %copy-start.3 = (s32[1,128]{1,0:T(1,128)S(1)}, s32[1,128]{1,0:T(1,128)}, u32[]{:S(2)}) copy-start(s32[1,128]{1,0:T(1,128)} %param.4) | copy-start | bytes 1540
  16.6 7.8 %collective-permute-start = (bf16[2,256,3072]{1,2,0:T(8,128)(2,1)}, bf16[2,256,3072]{1,2,0:T(8,128)(2,1)S(1)}, u32[]{:S(2)}, u32[]{:S(2)}) collective-permute-start(bf16[2,256,3072]{1,2,0:T(8,128)(2,1)} %slice.56), channel_id=1, source_target_pairs={{1,0},{2,1},{3,2},{4,3},{5,4},{6,5},{7,6},{9,8},{10,9},{11,10},{12... | collective-permute-start | bytes 9437192 | tf_op jit(solution)/shard_map/ppermute | solution.py:17
  52.4 4.1 %copy-start.1 = (bf16[1024,1024]{1,0:T(8,128)(2,1)S(1)}, bf16[1024,1024]{1,0:T(8,128)(2,1)}, u32[]{:S(2)}) copy-start(bf16[1024,1024]{1,0:T(8,128)(2,1)} %reshape_squeeze.7) | copy-start | bytes 6291460
  58.9 2.4 copy-start
  63.8 68.8 %copy-start.2 = (s32[128]{0:T(128)S(1)}, s32[128]{0:T(128)}, u32[]{:S(2)}) copy-start(s32[128]{0:T(128)} %param.5) | copy-start | bytes 1540
  139.5 64.9 %all-to-all-start = ((bf16[20,8,2,4,1024]{4,2,0,3,1:T(2,128)(2,1)}), bf16[20,8,2,4,1024]{4,2,0,3,1:T(2,128)(2,1)S(1)}, u32[]{:S(2)}, u32[]{:S(2)}) async-start(bf16[20,8,2,4,1024]{4,2,0,3,1:T(2,128)(2,1)} %copy.26), calls=%async_computation | async-start | bytes 5242880 | tf_op jit(solution)/shard_map/all_to_all | solution.py:85
Sparse Core Ops, SparseCore 0:
  64.9 67.6 all-gather.1
where the time goes:
time: 256 us; the launch traced here: 255 us
  waiting for transfers between devices  133 us (52%)
  local copies, waits for them, and re-layouts  37.8 us (15%)
  other arithmetic  33 us (13%)
  matrix products  31.4 us (12%)
  between operations  14.3 us (6%)
  starting transfers between devices  5.89 us (2%)
    all_gather x1, waiting for transfers between devices, body(): complete = lax.all_gather(spectra, 'feed', axis=3, tiled=True)  67.8 us
    all_to_all x1, waiting for transfers between devices, body(): lax.all_to_all(placed.reshape((CAP, owners) + complete.shape[1:]), 'freq'...  60.3 us
    convert_element_type x1, other arithmetic, correlate(): return (jnp.stack([real_vis, imag_vis], 1) * inverse).astype(jnp.bfloat16)  16.2 us
    convert_element_type x1, other arithmetic, channelize(): weighted = summed.astype(jnp.bfloat16)  9.16 us
    dot_general x1, matrix products, correlate(): jnp.einsum('cpzsf,cpzsg->cfg', own_rows, swapped, preferred_element_type=...  9.09 us
    dot_general x1, matrix products, correlate(): jnp.einsum('cpzsf,cpzsg->cfg', own_rows, columns, preferred_element_type=...  8.55 us
    convert_element_type x1, local copies, waits for them, and re-layouts, correlate(): return (jnp.stack([real_vis, imag_vis], 1) * inverse).astype(jnp.bfloat16)  7.34 us
    unnamed x9, local copies, waits for them, and re-layouts  6.34 us
  transfers between devices with their start and end apart: 3, of which 3 were waited for; matrix products, arithmetic and copies ran while one was open for 0% of the time, Pallas kernels for 0%

commit v1 on v0

v1 whole, which is shorter than its diff:
```python
import functools
import math

import jax
import jax.numpy as jnp
import ml_dtypes
import numpy as np
from jax import lax
from jax.experimental import pallas as pl
from jax.experimental.pallas import tpu as pltpu
from jax.sharding import PartitionSpec as P

CH = 1024
TAPS = 4
BAND_LO = 256
CAP = 20
QUAD = 4
GROUPS = CAP // QUAD
MESH = pl.DeviceIdType.MESH
MIB = 1024 * 1024


def prototype():
    total = TAPS * CH
    position = np.arange(total, dtype=np.float64)
    taper = 0.5 - 0.5 * np.cos(2 * np.pi * (position + 0.5) / total)
    coeffs = np.sinc((position - total / 2 + 0.5) / CH) * taper
    coeffs = coeffs * np.sqrt(CH / np.sum(coeffs * coeffs))
    return coeffs.reshape(TAPS, CH).astype(np.float32)


def tables(band):
    phase = (np.arange(band)[:, None] + BAND_LO) * np.arange(CH)[None, :] % CH * (2 * np.pi / CH)
    cosine = np.cos(phase).astype(np.float32).astype(ml_dtypes.bfloat16)
    sine = np.sin(phase).astype(np.float32).astype(ml_dtypes.bfloat16)
    return np.concatenate(
        [np.concatenate([cosine, sine], 1), np.concatenate([-sine, cosine], 1)], 0
    )


def spread_kernel(
    count, owners, voltage, coeffs, table, flags, owner_slot, gathered,
    slot_table, weighted, halo_out, halo_in, parts, outgoing,
    halo_send, halo_recv, local_sem, a_send, a_recv, x_send, x_recv, y_send, y_recv, d_send, d_recv,
):
    feed, me = lax.axis_index("feed"), lax.axis_index("freq")
    feeds = voltage.shape[1]
    band = flags.shape[1]
    rows = slot_table.shape[0]
    along_x, along_y = feed ^ 1, feed ^ 2

    barrier = pltpu.get_barrier_semaphore()
    for step in range(1, owners):
        pl.semaphore_signal(barrier, inc=1, device_id=(feed, me ^ step), device_id_type=MESH)
    for other in (along_x, along_y):
        pl.semaphore_signal(barrier, inc=1, device_id=(other, me), device_id_type=MESH)

    row = lax.broadcasted_iota(jnp.int32, (rows, band), 0)
    slot = row // (2 * QUAD) * QUAD + row % QUAD
    kept = jnp.where(slot == owner_slot[...], flags[...].astype(jnp.float32), 0.0)
    kept = kept * (1.0 / math.sqrt(CH))
    imag_row = row // QUAD % 2 == 1
    slot_table[...] = (
        jnp.dot(
            jnp.where(imag_row, 0.0, kept).astype(jnp.bfloat16),
            table[0:band, :],
            preferred_element_type=jnp.float32,
        )
        + jnp.dot(
            jnp.where(imag_row, kept, 0.0).astype(jnp.bfloat16),
            table[band : 2 * band, :],
            preferred_element_type=jnp.float32,
        )
    ).astype(jnp.bfloat16)

    def weigh(sums):
        tall = 32

        @pl.loop(0, feeds // tall)
        def _(index):
            here = pl.ds(pl.multiple_of(index * tall, tall), tall)
            for part in range(2):
                for lane in range(0, CH, 128):
                    blocks = [
                        voltage[part, here, block * CH + lane : block * CH + lane + 128].astype(jnp.float32)
                        for block in range(count)
                    ]
                    for place, pairs in enumerate(sums):
                        total = None
                        for tap, block in pairs:
                            term = blocks[block] * coeffs[tap : tap + 1, lane : lane + 128]
                            total = term if total is None else total + term
                        weighted[place, here, part * CH + lane : part * CH + lane + 128] = total.astype(
                            jnp.bfloat16
                        )

    def transform(place):
        return lax.dot_general(
            slot_table[...],
            weighted[place],
            (((1,), (1,)), ((), ())),
            preferred_element_type=jnp.float32,
        )

    halo = TAPS - 1
    weigh(
        [
            [(tap, spectrum + tap - count) for tap in range(TAPS) if 0 <= spectrum + tap - count < count]
            for spectrum in range(count - halo, count)
        ]
    )

    @pl.loop(0, halo)
    def _(place):
        halo_out[place] = transform(place).astype(jnp.bfloat16)

    pl.semaphore_wait(barrier, owners + 1)
    backward = pltpu.make_async_remote_copy(
        src_ref=halo_out,
        dst_ref=halo_in,
        send_sem=halo_send,
        recv_sem=halo_recv,
        device_id=(feed, jnp.maximum(me - 1, 0)),
        device_id_type=MESH,
    )

    @pl.when(me > 0)
    def _():
        backward.start()

    weigh(
        [
            [(tap, spectrum + tap) for tap in range(TAPS) if spectrum + tap < count]
            for spectrum in range(count)
        ]
    )

    @pl.loop(0, count)
    def _(place):
        parts[place] = transform(place)

    @pl.when(me < owners - 1)
    def _():
        backward.wait_recv()
        for place in range(halo):
            parts[count - halo + place] += halo_in[place].astype(jnp.float32)

    for place in range(0, count, 2):
        pair = [parts[place + k].reshape(rows // 8, 8, feeds) for k in range(2)]
        outgoing[:, place * 8 : place * 8 + 16, :] = jnp.concatenate(pair, 1).astype(jnp.bfloat16)

    def chunk(owner):
        return outgoing.at[pl.ds(owner * GROUPS, GROUPS)]

    keep = pltpu.make_async_copy(chunk(me), gathered.at[feed, me], local_sem)
    keep.start()

    def remote(source, target, send, recv, device):
        return pltpu.make_async_remote_copy(
            src_ref=source, dst_ref=target, send_sem=send, recv_sem=recv, device_id=device, device_id_type=MESH
        )

    to_owner = [None] + [
        remote(chunk(me ^ t), gathered.at[feed, me], a_send.at[t], a_recv.at[t], (feed, me ^ t))
        for t in range(1, owners)
    ]

    def shared(t):
        return chunk(me) if t == 0 else gathered.at[feed, me ^ t]

    to_x = [
        remote(shared(t), gathered.at[feed, me ^ t], x_send.at[t], x_recv.at[t], (along_x, me))
        for t in range(owners)
    ]
    to_y = [
        remote(shared(t), gathered.at[feed, me ^ t], y_send.at[t], y_recv.at[t], (along_y, me))
        for t in range(owners)
    ]
    onward = []
    for t in range(owners):
        origin, target = (along_x, along_y) if t % 2 else (along_y, along_x)
        block = gathered.at[origin, me ^ t]
        onward.append(remote(block, block, d_send.at[t], d_recv.at[t], (target, me)))

    def pass_on(t):
        (to_x if t % 2 else to_y)[t].wait_recv()
        onward[t].start()

    to_x[0].start()
    to_y[0].start()
    for t in range(1, owners):
        to_owner[t].start()
    for t in range(1, owners):
        to_owner[t].wait_recv()
        to_x[t].start()
        to_y[t].start()
        pass_on(t - 1)
    pass_on(owners - 1)

    keep.wait()
    for t in range(owners):
        (to_y if t % 2 else to_x)[t].wait_recv()
        onward[t].wait_recv()
        if t:
            to_owner[t].wait_send()
        to_x[t].wait_send()
        to_y[t].wait_send()
        onward[t].wait_send()

    @pl.when(me > 0)
    def _():
        backward.wait_send()


def spread(voltage, flags, owner_slot, feed_groups, owners):
    feeds, samples = voltage.shape[1:]
    band = flags.shape[1]
    count = samples // CH
    rows = owners * CAP * 2
    tall = count * 2 * QUAD
    vmem = pl.BlockSpec(memory_space=pltpu.VMEM)
    dma = pltpu.SemaphoreType.DMA
    return pl.pallas_call(
        functools.partial(spread_kernel, count, owners),
        out_shape=jax.ShapeDtypeStruct((feed_groups, owners, GROUPS, tall, feeds), jnp.bfloat16),
        in_specs=[vmem] * 5,
        out_specs=pl.BlockSpec(memory_space=pl.ANY),
        scratch_shapes=[
            pltpu.VMEM((rows, 2 * CH), jnp.bfloat16),
            pltpu.VMEM((count, feeds, 2 * CH), jnp.bfloat16),
            pltpu.VMEM((TAPS - 1, rows, feeds), jnp.bfloat16),
            pltpu.VMEM((TAPS - 1, rows, feeds), jnp.bfloat16),
            pltpu.VMEM((count, rows, feeds), jnp.float32),
            pltpu.VMEM((owners * GROUPS, tall, feeds), jnp.bfloat16),
            dma,
            dma,
            dma,
        ]
        + [dma((owners,))] * 8,
        compiler_params=pltpu.CompilerParams(
            collective_id=0, has_side_effects=True, vmem_limit_bytes=56 * MIB
        ),
    )(voltage, prototype(), tables(band), flags, owner_slot.reshape(1, band))


def correlate_kernel(inverse, gathered, out):
    feed_groups, owners, _, tall, feeds = gathered.shape
    depth = owners * tall
    first = pl.program_id(1) * out.shape[0]
    own = gathered[lax.axis_index("feed")].reshape(depth, feeds).T
    source = lax.broadcasted_iota(jnp.int32, (depth, depth), 0)
    target = lax.broadcasted_iota(jnp.int32, (depth, depth), 1)
    imag = target // QUAD % 2
    turn = jnp.where(
        source == target + QUAD - 2 * QUAD * imag, (2 * imag - 1).astype(jnp.float32), 0.0
    ).astype(jnp.bfloat16)
    turned = jnp.dot(own, turn, preferred_element_type=jnp.float32).astype(jnp.bfloat16)
    lane = lax.broadcasted_iota(jnp.int32, (1, depth), 1)
    for index in range(out.shape[0]):
        mask = jnp.where(lane % QUAD == first + index, inverse, 0.0).astype(jnp.bfloat16)
        for part, rows in enumerate((own, turned)):
            left = rows * mask
            for group in range(feed_groups):
                out[index, part, :, group * feeds : (group + 1) * feeds] = jnp.dot(
                    left, gathered[group].reshape(depth, feeds), preferred_element_type=jnp.float32
                ).astype(jnp.bfloat16)


def correlate(gathered):
    feed_groups, owners, _, tall, feeds = gathered.shape
    inverse = 1.0 / (owners * tall // (2 * QUAD))
    step = 2
    return pl.pallas_call(
        functools.partial(correlate_kernel, inverse),
        out_shape=jax.ShapeDtypeStruct((CAP, 2, feeds, feed_groups * feeds), jnp.bfloat16),
        grid=(GROUPS, QUAD // step),
        in_specs=[
            pl.BlockSpec((feed_groups, owners, 1, tall, feeds), lambda g, h: (0, 0, g, 0, 0))
        ],
        out_specs=pl.BlockSpec(
            (step, 2, feeds, feed_groups * feeds), lambda g, h: (g * (QUAD // step) + h, 0, 0, 0)
        ),
        compiler_params=pltpu.CompilerParams(vmem_limit_bytes=48 * MIB),
    )(gathered)


def solution(mesh):
    feed_groups, owners = mesh.shape["feed"], mesh.shape["freq"]

    def body(voltage, flags, owner_slot):
        return correlate(spread(voltage, flags, owner_slot, feed_groups, owners))

    placed = (P(None, "feed", "freq"), P("feed", None), P())
    return jax.shard_map(
        body, mesh=mesh, in_specs=placed, out_specs=P("freq", None, "feed", None), check_vma=False
    )
```

time: 256 us -> 56.9 us (0.22)
  waiting for transfers between devices: 133 us -> 0 us
  Pallas kernels: 0 us -> 55 us
  local copies, waits for them, and re-layouts: 37.8 us -> 1.73 us
  other arithmetic: 33 us -> 0 us
  matrix products: 31.4 us -> 0 us
  between operations: 14.3 us -> 0.02 us
  starting transfers between devices: 5.89 us -> 0 us
    all_gather x1 -> x0, waiting for transfers between devices: 67.8 us -> none  [body(): complete = lax.all_gather(spectra, 'feed', axis=3, tiled=True)]
    all_to_all x1 -> x0, waiting for transfers between devices: 60.3 us -> none  [body(): lax.all_to_all(placed.reshape((CAP, owners) + complete.shape[1:]), 'freq'...]
    pallas_call x0 -> x2, Pallas kernels: none -> 55 us  [the longest x1 43.4 us: spread(): pl.pallas_call(functools.partial(spread_kernel, count, owners), out_shape...]
    dot_general x7 -> x0, matrix products: 31.4 us -> none  [the longest x1 9.09 us: correlate(): jnp.einsum('cpzsf,cpzsg->cfg', own_rows, swapped, preferred_element_type=...]
    convert_element_type x3 -> x0, other arithmetic: 26.2 us -> none  [the longest x1 16.2 us: correlate(): return (jnp.stack([real_vis, imag_vis], 1) * inverse).astype(jnp.bfloat16)]
    slice x5 -> x0, local copies, waits for them, and re-layouts: 12.8 us -> none  [the longest x2 5.67 us: channelize(): real_rows = weighted[0].reshape(feeds * count, CH)]
    convert_element_type x1 -> x0, local copies, waits for them, and re-layouts: 7.34 us -> none  [correlate(): return (jnp.stack([real_vis, imag_vis], 1) * inverse).astype(jnp.bfloat16)]
    concatenate x1 -> x0, other arithmetic: 5.71 us -> none  [channelize(): longer = jnp.concatenate([voltage, extra], 2)]
  transfers between devices with their start and end apart: 3 -> 0, of which waited for: 3 -> 0; matrix products, arithmetic and copies ran while one was open for 0% -> 0% of each run, Pallas kernels for 0% -> 0%
where the time goes in v1:
time: 56.9 us; the launch traced here: 56.8 us
  Pallas kernels  55 us (97%)
  local copies, waits for them, and re-layouts  1.73 us (3%)
    pallas_call x1, Pallas kernels, spread(): pl.pallas_call(functools.partial(spread_kernel, count, owners), out_shape...  43.4 us
    pallas_call x1, Pallas kernels, correlate(): pl.pallas_call(functools.partial(correlate_kernel, inverse), out_shape=ja...  11.6 us
    unnamed x2, local copies, waits for them, and re-layouts  1.73 us

profile of v1, /device:TPU:0, one launch (start us, length us, event | category | flops | bytes accessed | tf_op | source)
XLA Modules:
  0.0 56.8 jit_solution(1126452989346685532)
XLA Ops:
  0.0 43.4 %shard_map.55.gathered = bf16[4,8,5,32,256]{4,3,2,1,0:T(8,128)(2,1)} custom-call(bf16[2,256,4096]{2,1,0:T(8,128)(2,1)} %voltage.1, f32[4,1024]{1,0:T(4,128)} %constant.4.clone.coeffs, bf16[256,2048]{1,0:T(8,128)(2,1)} %constant.5.clone.table, s32[1,128]{1,0:T(1,128)} %flags.1, s32[1,128]{1,0:T(1,128)} %bitcast.1), custom_call_target="tpu_custom_call" | custom-call | tf_op jit(solution)/shard_map/pallas_call | solution.py:223
  43.4 0.0 copy-start
  43.5 1.7 %copy-done = bf16[4,8,5,32,256]{4,3,2,1,0:T(8,128)(2,1)S(1)} copy-done((bf16[4,8,5,32,256]{4,3,2,1,0:T(8,128)(2,1)S(1)}, bf16[4,8,5,32,256]{4,3,2,1,0:T(8,128)(2,1)}, u32[]{:S(2)}) %copy-start) | copy-done | bytes 2621464
  45.2 11.6 %shard_map.56 = bf16[20,2,256,1024]{3,2,1,0:T(8,128)(2,1)} custom-call(bf16[4,8,5,32,256]{4,3,2,1,0:T(8,128)(2,1)S(1)} %copy-done), custom_call_target="tpu_custom_call" | custom-call | tf_op jit(solution)/shard_map/pallas_call | solution.py:273
Async XLA Ops:
  43.4 1.7 %copy-start = (bf16[4,8,5,32,256]{4,3,2,1,0:T(8,128)(2,1)S(1)}, bf16[4,8,5,32,256]{4,3,2,1,0:T(8,128)(2,1)}, u32[]{:S(2)}) copy-start(bf16[4,8,5,32,256]{4,3,2,1,0:T(8,128)(2,1)} %shard_map.55.gathered) | copy-start | bytes 7864324

commit v2 on v1

--- a/solution.py
+++ b/solution.py
@@ -243,32 +243,44 @@
     )(voltage, prototype(), tables(band), flags, owner_slot.reshape(1, band))
 
 
-def correlate_kernel(inverse, gathered, out):
+def correlate_kernel(inverse, gathered, out, turn, bases, lefts):
     feed_groups, owners, _, tall, feeds = gathered.shape
     depth = owners * tall
-    first = pl.program_id(1) * out.shape[0]
-    own = gathered[lax.axis_index("feed")].reshape(depth, feeds).T
-    source = lax.broadcasted_iota(jnp.int32, (depth, depth), 0)
-    target = lax.broadcasted_iota(jnp.int32, (depth, depth), 1)
-    imag = target // QUAD % 2
-    turn = jnp.where(
-        source == target + QUAD - 2 * QUAD * imag, (2 * imag - 1).astype(jnp.float32), 0.0
-    ).astype(jnp.bfloat16)
-    turned = jnp.dot(own, turn, preferred_element_type=jnp.float32).astype(jnp.bfloat16)
+    step = out.shape[0]
+    group_id, part_id = pl.program_id(0), pl.program_id(1)
+
+    @pl.when((group_id == 0) & (part_id == 0))
+    def _():
+        source = lax.broadcasted_iota(jnp.int32, (depth, depth), 0)
+        target = lax.broadcasted_iota(jnp.int32, (depth, depth), 1)
+        imag = target // QUAD % 2
+        turn[...] = jnp.where(
+            source == target + QUAD - 2 * QUAD * imag, (2 * imag - 1).astype(jnp.float32), 0.0
+        ).astype(jnp.bfloat16)
+
+    @pl.when(part_id == 0)
+    def _():
+        own = gathered[lax.axis_index("feed")].reshape(depth, feeds).T
+        bases[0] = own
+        bases[1] = jnp.dot(own, turn[...], preferred_element_type=jnp.float32).astype(jnp.bfloat16)
+
     lane = lax.broadcasted_iota(jnp.int32, (1, depth), 1)
-    for index in range(out.shape[0]):
-        mask = jnp.where(lane % QUAD == first + index, inverse, 0.0).astype(jnp.bfloat16)
-        for part, rows in enumerate((own, turned)):
-            left = rows * mask
-            for group in range(feed_groups):
-                out[index, part, :, group * feeds : (group + 1) * feeds] = jnp.dot(
-                    left, gathered[group].reshape(depth, feeds), preferred_element_type=jnp.float32
-                ).astype(jnp.bfloat16)
+    for index in range(step):
+        mask = jnp.where(lane % QUAD == part_id * step + index, inverse, 0.0).astype(jnp.bfloat16)
+        for part in range(2):
+            lefts[index, part] = bases[part] * mask
+    left = lefts[...].reshape(step * 2 * feeds, depth)
+    for group in range(feed_groups):
+        product = jnp.dot(left, gathered[group].reshape(depth, feeds), preferred_element_type=jnp.float32)
+        out[:, :, :, group * feeds : (group + 1) * feeds] = product.astype(jnp.bfloat16).reshape(
+            step, 2, feeds, feeds
+        )
 
 
 def correlate(gathered):
     feed_groups, owners, _, tall, feeds = gathered.shape
-    inverse = 1.0 / (owners * tall // (2 * QUAD))
+    depth = owners * tall
+    inverse = 1.0 / (depth // (2 * QUAD))
     step = 2
     return pl.pallas_call(
         functools.partial(correlate_kernel, inverse),
@@ -280,7 +292,12 @@
         out_specs=pl.BlockSpec(
             (step, 2, feeds, feed_groups * feeds), lambda g, h: (g * (QUAD // step) + h, 0, 0, 0)
         ),
-        compiler_params=pltpu.CompilerParams(vmem_limit_bytes=48 * MIB),
+        scratch_shapes=[
+            pltpu.VMEM((depth, depth), jnp.bfloat16),
+            pltpu.VMEM((2, feeds, depth), jnp.bfloat16),
+            pltpu.VMEM((step, 2, feeds, depth), jnp.bfloat16),
+        ],
+        compiler_params=pltpu.CompilerParams(vmem_limit_bytes=62 * MIB),
     )(gathered)
 
 

time: 56.9 us -> 57.5 us (1.011)
  Pallas kernels: 55 us -> 57.2 us
  local copies, waits for them, and re-layouts: 1.73 us -> 0 us
    pallas_call x1, Pallas kernels: 11.6 us -> 13.8 us  [correlate(): pl.pallas_call(functools.partial(correlate_kernel, inverse), out_shape=ja...]
    unnamed x2 -> x0, local copies, waits for them, and re-layouts: 1.73 us -> none
where the time goes in v2:
time: 57.5 us; the launch traced here: 57.2 us
  Pallas kernels  57.2 us (99%)
    pallas_call x1, Pallas kernels, spread(): pl.pallas_call(functools.partial(spread_kernel, count, owners), out_shape...  43.4 us
    pallas_call x1, Pallas kernels, correlate(): pl.pallas_call(functools.partial(correlate_kernel, inverse), out_shape=ja...  13.8 us

profile of v2, /device:TPU:0, one launch (start us, length us, event | category | flops | bytes accessed | tf_op | source)
XLA Modules:
  0.0 57.2 jit_solution(952826232729941769)
XLA Ops:
  0.0 43.4 %shard_map.55.gathered = bf16[4,8,5,32,256]{4,3,2,1,0:T(8,128)(2,1)} custom-call(bf16[2,256,4096]{2,1,0:T(8,128)(2,1)} %voltage.1, f32[4,1024]{1,0:T(4,128)} %constant.4.clone.coeffs, bf16[256,2048]{1,0:T(8,128)(2,1)} %constant.5.clone.table, s32[1,128]{1,0:T(1,128)} %flags.1, s32[1,128]{1,0:T(1,128)} %bitcast.1), custom_call_target="tpu_custom_call" | custom-call | tf_op jit(solution)/shard_map/pallas_call | solution.py:223
  43.4 13.8 %shard_map.56 = bf16[20,2,256,1024]{3,2,1,0:T(8,128)(2,1)} custom-call(bf16[4,8,5,32,256]{4,3,2,1,0:T(8,128)(2,1)} %shard_map.55.gathered), custom_call_target="tpu_custom_call" | custom-call | tf_op jit(solution)/shard_map/pallas_call | solution.py:285

commit v3 on v2

v3 whole, which is shorter than its diff:
```python
import functools
import math

import jax
import jax.numpy as jnp
import ml_dtypes
import numpy as np
from jax import lax
from jax.experimental import pallas as pl
from jax.experimental.pallas import tpu as pltpu
from jax.sharding import PartitionSpec as P

CH = 1024
TAPS = 4
BAND_LO = 256
CAP = 20
QUAD = 4
GROUPS = CAP // QUAD
HALVES = 2
MESH = pl.DeviceIdType.MESH
MIB = 1024 * 1024


def prototype():
    total = TAPS * CH
    position = np.arange(total, dtype=np.float64)
    taper = 0.5 - 0.5 * np.cos(2 * np.pi * (position + 0.5) / total)
    coeffs = np.sinc((position - total / 2 + 0.5) / CH) * taper
    coeffs = coeffs * np.sqrt(CH / np.sum(coeffs * coeffs))
    return coeffs.reshape(TAPS, CH).astype(np.float32)


def tables(band):
    phase = (np.arange(band)[:, None] + BAND_LO) * np.arange(CH)[None, :] % CH * (2 * np.pi / CH)
    cosine = np.cos(phase).astype(np.float32).astype(ml_dtypes.bfloat16)
    sine = np.sin(phase).astype(np.float32).astype(ml_dtypes.bfloat16)
    return np.concatenate([cosine, sine], 0)


def spread_kernel(
    count, owners, voltage, coeffs, table, flags, owner_slot, gathered,
    samples, slot_table, weighted, halo_out, halo_in, parts, outgoing,
    load_sem, halo_send, halo_recv, local_sem,
    a_send, a_recv, x_send, x_recv, y_send, y_recv, d_send, d_recv,
):
    feed, me = lax.axis_index("feed"), lax.axis_index("freq")
    feeds = samples.shape[2]
    band = flags.shape[1]
    rows = slot_table.shape[0]
    along_x, along_y = feed ^ 1, feed ^ 2
    halo = TAPS - 1

    barrier = pltpu.get_barrier_semaphore()
    for step in range(1, owners):
        pl.semaphore_signal(barrier, inc=1, device_id=(feed, me ^ step), device_id_type=MESH)
    for other in (along_x, along_y):
        pl.semaphore_signal(barrier, inc=1, device_id=(other, me), device_id_type=MESH)

    loads = [
        pltpu.make_async_copy(
            voltage.at[:, half * feeds : (half + 1) * feeds, :], samples.at[half], load_sem.at[half]
        )
        for half in range(HALVES)
    ]
    for load in loads:
        load.start()

    row = lax.broadcasted_iota(jnp.int32, (rows, band), 0)
    slot = row // (2 * QUAD) * QUAD + row % QUAD
    kept = jnp.where(slot == owner_slot[...], flags[...].astype(jnp.float32), 0.0)
    kept = kept * (1.0 / math.sqrt(CH))
    imag_row = row // QUAD % 2 == 1
    real_kept = jnp.where(imag_row, 0.0, kept)
    imag_kept = jnp.where(imag_row, kept, 0.0)
    for part, pick in enumerate(([real_kept, -imag_kept], [imag_kept, real_kept])):
        slot_table[:, part * CH : (part + 1) * CH] = jnp.dot(
            jnp.concatenate(pick, 1).astype(jnp.bfloat16), table[...], preferred_element_type=jnp.float32
        ).astype(jnp.bfloat16)

    def weigh(half, sums):
        tall = 32

        @pl.loop(0, feeds // tall)
        def _(index):
            first = pl.multiple_of(index * tall, tall)
            for part in range(2):
                for lane in range(0, CH, 128):
                    blocks = [
                        samples[
                            half, part, pl.ds(first, tall), block * CH + lane : block * CH + lane + 128
                        ].astype(jnp.float32)
                        for block in range(count)
                    ]
                    for place, pairs in enumerate(sums):
                        total = None
                        for tap, block in pairs:
                            term = blocks[block] * coeffs[tap : tap + 1, lane : lane + 128]
                            total = term if total is None else total + term
                        weighted[
                            pl.ds(place * feeds + first, tall), part * CH + lane : part * CH + lane + 128
                        ] = total.astype(jnp.bfloat16)

    def transform(places):
        return lax.dot_general(
            slot_table[...],
            weighted[0 : places * feeds, :],
            (((1,), (1,)), ((), ())),
            preferred_element_type=jnp.float32,
        )

    def backward(half):
        return pltpu.make_async_remote_copy(
            src_ref=halo_out.at[half],
            dst_ref=halo_in.at[half],
            send_sem=halo_send.at[half],
            recv_sem=halo_recv.at[half],
            device_id=(feed, jnp.maximum(me - 1, 0)),
            device_id_type=MESH,
        )

    def send_halo(half):
        weigh(
            half,
            [
                [(tap, spectrum + tap - count) for tap in range(TAPS) if 0 <= spectrum + tap - count < count]
                for spectrum in range(count - halo, count)
            ],
        )
        halo_out[half] = transform(halo).astype(jnp.bfloat16)
        if half == 0:
            pl.semaphore_wait(barrier, owners + 1)

        @pl.when(me > 0)
        def _():
            backward(half).start()

    def channelize(half):
        weigh(
            half,
            [
                [(tap, spectrum + tap) for tap in range(TAPS) if spectrum + tap < count]
                for spectrum in range(count)
            ],
        )
        parts[...] = transform(count)

    def finish(half):
        @pl.when(me < owners - 1)
        def _():
            backward(half).wait_recv()
            parts[:, (count - halo) * feeds :] += halo_in[half].astype(jnp.float32)

        for place in range(0, count, 2):
            pair = [
                parts[:, (place + k) * feeds : (place + k + 1) * feeds].reshape(rows // 8, 8, feeds)
                for k in range(2)
            ]
            outgoing[half, :, place * 8 : place * 8 + 16, :] = jnp.concatenate(pair, 1).astype(jnp.bfloat16)

    def chunk(half, owner):
        return outgoing.at[half, pl.ds(owner * GROUPS, GROUPS)]

    def remote(source, target, send, recv, device):
        return pltpu.make_async_remote_copy(
            src_ref=source, dst_ref=target, send_sem=send, recv_sem=recv, device_id=device, device_id_type=MESH
        )

    def keep(half):
        return pltpu.make_async_copy(chunk(half, me), gathered.at[feed, half, me], local_sem.at[half])

    def to_owner(half, t):
        return remote(
            chunk(half, me ^ t), gathered.at[feed, half, me],
            a_send.at[half, t], a_recv.at[half, t], (feed, me ^ t),
        )

    def shared(half, t):
        return chunk(half, me) if t == 0 else gathered.at[feed, half, me ^ t]

    def to_x(half, t):
        return remote(
            shared(half, t), gathered.at[feed, half, me ^ t],
            x_send.at[half, t], x_recv.at[half, t], (along_x, me),
        )

    def to_y(half, t):
        return remote(
            shared(half, t), gathered.at[feed, half, me ^ t],
            y_send.at[half, t], y_recv.at[half, t], (along_y, me),
        )

    def onward(half, t):
        origin, target = (along_x, along_y) if t % 2 else (along_y, along_x)
        block = gathered.at[origin, half, me ^ t]
        return remote(block, block, d_send.at[half, t], d_recv.at[half, t], (target, me))

    def pass_on(half, t):
        (to_x if t % 2 else to_y)(half, t).wait_recv()
        onward(half, t).start()

    def send(half):
        to_x(half, 0).start()
        to_y(half, 0).start()
        for t in range(1, owners):
            to_owner(half, t).start()
        keep(half).start()

    loads[0].wait()
    send_halo(0)
    channelize(0)
    loads[1].wait()
    send_halo(1)
    finish(0)
    send(0)
    channelize(1)
    finish(1)
    send(1)

    steps = [(half, t) for half in range(HALVES) for t in range(owners)]
    for before, (half, t) in zip([None] + steps, steps):
        if t:
            to_owner(half, t).wait_recv()
            to_x(half, t).start()
            to_y(half, t).start()
        if before:
            pass_on(*before)
    pass_on(*steps[-1])

    for half, t in steps:
        (to_y if t % 2 else to_x)(half, t).wait_recv()
        onward(half, t).wait_recv()
        if t:
            to_owner(half, t).wait_send()
        to_x(half, t).wait_send()
        to_y(half, t).wait_send()
        onward(half, t).wait_send()
    for half in range(HALVES):
        keep(half).wait()

        @pl.when(me > 0)
        def _():
            backward(half).wait_send()


def spread(voltage, flags, owner_slot, feed_groups, owners):
    feeds, samples = voltage.shape[1:]
    feeds = feeds // HALVES
    band = flags.shape[1]
    count = samples // CH
    rows = owners * CAP * 2
    tall = count * 2 * QUAD
    vmem, anywhere = pl.BlockSpec(memory_space=pltpu.VMEM), pl.BlockSpec(memory_space=pl.ANY)
    dma = pltpu.SemaphoreType.DMA
    return pl.pallas_call(
        functools.partial(spread_kernel, count, owners),
        out_shape=jax.ShapeDtypeStruct(
            (feed_groups, HALVES, owners, GROUPS, tall, feeds), jnp.bfloat16
        ),
        in_specs=[anywhere] + [vmem] * 4,
        out_specs=anywhere,
        scratch_shapes=[
            pltpu.VMEM((HALVES, 2, feeds, samples), jnp.bfloat16),
            pltpu.VMEM((rows, 2 * CH), jnp.bfloat16),
            pltpu.VMEM((count * feeds, 2 * CH), jnp.bfloat16),
            pltpu.VMEM((HALVES, rows, (TAPS - 1) * feeds), jnp.bfloat16),
            pltpu.VMEM((HALVES, rows, (TAPS - 1) * feeds), jnp.bfloat16),
            pltpu.VMEM((rows, count * feeds), jnp.float32),
            pltpu.VMEM((HALVES, owners * GROUPS, tall, feeds), jnp.bfloat16),
        ]
        + [dma((HALVES,))] * 4
        + [dma((HALVES, owners))] * 8,
        compiler_params=pltpu.CompilerParams(
            collective_id=0, has_side_effects=True, vmem_limit_bytes=62 * MIB
        ),
    )(voltage, prototype(), tables(band), flags, owner_slot.reshape(1, band))


def correlate_kernel(inverse, gathered, out, turn, bases):
    feed_groups, halves, owners, _, tall, some = gathered.shape
    depth, feeds = owners * tall, halves * some
    step = out.shape[0]
    group_id, part_id = pl.program_id(0), pl.program_id(1)

    @pl.when((group_id == 0) & (part_id == 0))
    def _():
        source = lax.broadcasted_iota(jnp.int32, (depth, depth), 0)
        target = lax.broadcasted_iota(jnp.int32, (depth, depth), 1)
        imag = target // QUAD % 2
        turn[...] = jnp.where(
            source == target + QUAD - 2 * QUAD * imag, (2 * imag - 1).astype(jnp.float32), 0.0
        ).astype(jnp.bfloat16)

    @pl.when(part_id == 0)
    def _():
        mine = lax.axis_index("feed")
        own = jnp.concatenate([gathered[mine, half].reshape(depth, some).T for half in range(halves)], 0)
        bases[0] = own
        bases[1] = jnp.dot(own, turn[...], preferred_element_type=jnp.float32).astype(jnp.bfloat16)

    lane = lax.broadcasted_iota(jnp.int32, (1, depth), 1)
    right = jnp.concatenate(
        [gathered[group, half].reshape(depth, some) for group in range(feed_groups) for half in range(halves)], 1
    )
    for index in range(step):
        mask = jnp.where(lane % QUAD == part_id * step + index, inverse, 0.0).astype(jnp.bfloat16)
        for part in range(2):
            out[index, part] = jnp.dot(
                bases[part] * mask, right, preferred_element_type=jnp.float32
            ).astype(jnp.bfloat16)


def correlate(gathered):
    feed_groups, halves, owners, _, tall, some = gathered.shape
    depth, feeds = owners * tall, halves * some
    inverse = 1.0 / (depth // (2 * QUAD))
    step = 2
    return pl.pallas_call(
        functools.partial(correlate_kernel, inverse),
        out_shape=jax.ShapeDtypeStruct((CAP, 2, feeds, feed_groups * feeds), jnp.bfloat16),
        grid=(GROUPS, QUAD // step),
        in_specs=[
            pl.BlockSpec((feed_groups, halves, owners, 1, tall, some), lambda g, h: (0, 0, 0, g, 0, 0))
        ],
        out_specs=pl.BlockSpec(
            (step, 2, feeds, feed_groups * feeds), lambda g, h: (g * (QUAD // step) + h, 0, 0, 0)
        ),
        scratch_shapes=[
            pltpu.VMEM((depth, depth), jnp.bfloat16),
            pltpu.VMEM((2, feeds, depth), jnp.bfloat16),
        ],
        compiler_params=pltpu.CompilerParams(vmem_limit_bytes=62 * MIB),
    )(gathered)


def solution(mesh):
    feed_groups, owners = mesh.shape["feed"], mesh.shape["freq"]

    def body(voltage, flags, owner_slot):
        return correlate(spread(voltage, flags, owner_slot, feed_groups, owners))

    placed = (P(None, "feed", "freq"), P("feed", None), P())
    return jax.shard_map(
        body, mesh=mesh, in_specs=placed, out_specs=P("freq", None, "feed", None), check_vma=False
    )
```

time: 57.5 us -> 61.9 us (1.077); the launches traced: 57.2 us -> 60.9 us
  Pallas kernels: 57.2 us -> 60.9 us
    pallas_call x1, Pallas kernels: 43.4 us -> 47 us  [spread(): pl.pallas_call(functools.partial(spread_kernel, count, owners), out_shape...]
where the time goes in v3:
time: 61.9 us; the launch traced here: 60.9 us
  Pallas kernels  60.9 us (98%)
    pallas_call x1, Pallas kernels, spread(): pl.pallas_call(functools.partial(spread_kernel, count, owners), out_shape...  47 us
    pallas_call x1, Pallas kernels, correlate(): pl.pallas_call(functools.partial(correlate_kernel, inverse), out_shape=ja...  13.9 us

profile of v3, /device:TPU:0, one launch (start us, length us, event | category | flops | bytes accessed | tf_op | source)
XLA Modules:
  0.0 60.9 jit_solution(4380406107485541154)
XLA Ops:
  0.0 47.0 %shard_map.55.gathered = bf16[4,2,8,5,32,128]{5,4,3,2,1,0:T(8,128)(2,1)} custom-call(bf16[2,256,4096]{2,1,0:T(8,128)(2,1)} %voltage.1, f32[4,1024]{1,0:T(4,128)} %constant.4.clone.coeffs, bf16[256,1024]{1,0:T(8,128)(2,1)} %constant.5.clone.table, s32[1,128]{1,0:T(1,128)} %flags.1, s32[1,128]{1,0:T(1,128)} %bitcast.1), custom_call_target="tpu_custom_call" | custom-call | tf_op jit(solution)/shard_map/pallas_call | solution.py:254
  47.0 13.9 %shard_map.56 = bf16[20,2,256,1024]{3,2,1,0:T(8,128)(2,1)} custom-call(bf16[4,2,8,5,32,128]{5,4,3,2,1,0:T(8,128)(2,1)} %shard_map.55.gathered), custom_call_target="tpu_custom_call" | custom-call | tf_op jit(solution)/shard_map/pallas_call | solution.py:317

commit v4 on v3

--- a/solution.py
+++ b/solution.py
@@ -17,6 +17,9 @@
 QUAD = 4
 GROUPS = CAP // QUAD
 HALVES = 2
+LAG = 3
+WINDOW = 4
+DEPTH = 2
 MESH = pl.DeviceIdType.MESH
 MIB = 1024 * 1024
 
@@ -134,7 +137,7 @@
         def _():
             backward(half).start()
 
-    def channelize(half):
+    def weigh_own(half):
         weigh(
             half,
             [
@@ -142,6 +145,8 @@
                 for spectrum in range(count)
             ],
         )
+
+    def transform_own():
         parts[...] = transform(count)
 
     def finish(half):
@@ -198,33 +203,62 @@
         (to_x if t % 2 else to_y)(half, t).wait_recv()
         onward(half, t).start()
 
-    def send(half):
-        to_x(half, 0).start()
-        to_y(half, 0).start()
-        for t in range(1, owners):
-            to_owner(half, t).start()
-        keep(half).start()
+    steps = sorted(
+        [(half, t) for half in range(HALVES) for t in range(owners)],
+        key=lambda step: (step[1] + LAG * step[0], -step[0]),
+    )
+    early = [(0, t) for t in range(min(LAG + 1, owners))] if HALVES > 1 else []
+    steps = early + [step for step in steps if step not in early]
+    leaving = [step for step in steps if step[1]]
+    handled = []
+
+    def leave(half, limit):
+        ready = [step for step in leaving if step[0] <= half][:limit]
+        for step in ready:
+            leaving.remove(step)
+            to_owner(*step).start()
+
+    def handle(step, ready):
+        half, t = step
+        if t:
+            assert step not in leaving
+            to_owner(half, t).wait_recv()
+            leave(ready, 1)
+        to_x(half, t).start()
+        to_y(half, t).start()
+        handled.append(step)
+        if len(handled) > DEPTH:
+            pass_on(*handled[-1 - DEPTH])
 
     loads[0].wait()
     send_halo(0)
-    channelize(0)
-    loads[1].wait()
-    send_halo(1)
+    weigh_own(0)
+    transform_own()
+    for half in range(1, HALVES):
+        loads[half].wait()
+        send_halo(half)
     finish(0)
-    send(0)
-    channelize(1)
-    finish(1)
-    send(1)
-
-    steps = [(half, t) for half in range(HALVES) for t in range(owners)]
-    for before, (half, t) in zip([None] + steps, steps):
-        if t:
-            to_owner(half, t).wait_recv()
-            to_x(half, t).start()
-            to_y(half, t).start()
-        if before:
-            pass_on(*before)
-    pass_on(*steps[-1])
+    keep(0).start()
+    if HALVES == 1:
+        handle(steps[0], 0)
+        leave(0, WINDOW)
+    else:
+        handle(early[0], 0)
+        leave(0, WINDOW)
+        weigh_own(1)
+        handle(early[1], 0)
+        transform_own()
+        for step in early[2:]:
+            handle(step, 0)
+        finish(1)
+        keep(1).start()
+        handle((1, 0), 1)
+        leave(1, WINDOW)
+    for step in steps:
+        if step not in handled:
+            handle(step, HALVES - 1)
+    for step in handled[-DEPTH:]:
+        pass_on(*step)
 
     for half, t in steps:
         (to_y if t % 2 else to_x)(half, t).wait_recv()
@@ -275,58 +309,70 @@
     )(voltage, prototype(), tables(band), flags, owner_slot.reshape(1, band))
 
 
-def correlate_kernel(inverse, gathered, out, turn, bases):
-    feed_groups, halves, owners, _, tall, some = gathered.shape
-    depth, feeds = owners * tall, halves * some
-    step = out.shape[0]
-    group_id, part_id = pl.program_id(0), pl.program_id(1)
-
-    @pl.when((group_id == 0) & (part_id == 0))
-    def _():
-        source = lax.broadcasted_iota(jnp.int32, (depth, depth), 0)
-        target = lax.broadcasted_iota(jnp.int32, (depth, depth), 1)
-        imag = target // QUAD % 2
-        turn[...] = jnp.where(
-            source == target + QUAD - 2 * QUAD * imag, (2 * imag - 1).astype(jnp.float32), 0.0
-        ).astype(jnp.bfloat16)
-
-    @pl.when(part_id == 0)
-    def _():
-        mine = lax.axis_index("feed")
-        own = jnp.concatenate([gathered[mine, half].reshape(depth, some).T for half in range(halves)], 0)
+def correlate_kernel(inverse, gathered, out, held, turn, bases, results, in_sem, out_sem):
+    _, feed_groups, halves, owners, tall, some = held.shape
+    depth = owners * tall
+
+    def fetch(group):
+        return pltpu.make_async_copy(gathered.at[:, :, :, group], held.at[group], in_sem.at[group])
+
+    def store(slot, part):
+        return pltpu.make_async_copy(results.at[slot, part], out.at[slot, part], out_sem.at[slot, part])
+
+    for group in range(GROUPS):
+        fetch(group).start()
+    source = lax.broadcasted_iota(jnp.int32, (depth, depth), 0)
+    target = lax.broadcasted_iota(jnp.int32, (depth, depth), 1)
+    imag = target // QUAD % 2
+    turn[...] = jnp.where(
+        source == target + QUAD - 2 * QUAD * imag, (2 * imag - 1).astype(jnp.float32), 0.0
+    ).astype(jnp.bfloat16)
+    lane = lax.broadcasted_iota(jnp.int32, (1, depth), 1)
+    mine = lax.axis_index("feed")
+
+    @pl.loop(0, GROUPS)
+    def _(group):
+        fetch(group).wait()
+        own = jnp.concatenate([held[group, mine, half].reshape(depth, some).T for half in range(halves)], 0)
         bases[0] = own
         bases[1] = jnp.dot(own, turn[...], preferred_element_type=jnp.float32).astype(jnp.bfloat16)
-
-    lane = lax.broadcasted_iota(jnp.int32, (1, depth), 1)
-    right = jnp.concatenate(
-        [gathered[group, half].reshape(depth, some) for group in range(feed_groups) for half in range(halves)], 1
-    )
-    for index in range(step):
-        mask = jnp.where(lane % QUAD == part_id * step + index, inverse, 0.0).astype(jnp.bfloat16)
+        right = jnp.concatenate(
+            [held[group, other, half].reshape(depth, some) for other in range(feed_groups) for half in range(halves)],
+            1,
+        )
+        for index in range(QUAD):
+            slot = group * QUAD + index
+            mask = jnp.where(lane % QUAD == index, inverse, 0.0).astype(jnp.bfloat16)
+            for part in range(2):
+                results[slot, part] = jnp.dot(
+                    bases[part] * mask, right, preferred_element_type=jnp.float32
+                ).astype(jnp.bfloat16)
+                store(slot, part).start()
+
+    @pl.loop(0, CAP)
+    def _(slot):
         for part in range(2):
-            out[index, part] = jnp.dot(
-                bases[part] * mask, right, preferred_element_type=jnp.float32
-            ).astype(jnp.bfloat16)
+            store(slot, part).wait()
 
 
 def correlate(gathered):
     feed_groups, halves, owners, _, tall, some = gathered.shape
     depth, feeds = owners * tall, halves * some
     inverse = 1.0 / (depth // (2 * QUAD))
-    step = 2
+    shape = (CAP, 2, feeds, feed_groups * feeds)
+    anywhere = pl.BlockSpec(memory_space=pl.ANY)
     return pl.pallas_call(
         functools.partial(correlate_kernel, inverse),
-        out_shape=jax.ShapeDtypeStruct((CAP, 2, feeds, feed_groups * feeds), jnp.bfloat16),
-        grid=(GROUPS, QUAD // step),
-        in_specs=[
-            pl.BlockSpec((feed_groups, halves, owners, 1, tall, some), lambda g, h: (0, 0, 0, g, 0, 0))
-        ],
-        out_specs=pl.BlockSpec(
-            (step, 2, feeds, feed_groups * feeds), lambda g, h: (g * (QUAD // step) + h, 0, 0, 0)
-        ),
+        out_shape=jax.ShapeDtypeStruct(shape, jnp.bfloat16),
+        in_specs=[anywhere],
+        out_specs=anywhere,
         scratch_shapes=[
+            pltpu.VMEM((GROUPS, feed_groups, halves, owners, tall, some), jnp.bfloat16),
             pltpu.VMEM((depth, depth), jnp.bfloat16),
             pltpu.VMEM((2, feeds, depth), jnp.bfloat16),
+            pltpu.VMEM(shape, jnp.bfloat16),
+            pltpu.SemaphoreType.DMA((GROUPS,)),
+            pltpu.SemaphoreType.DMA((CAP, 2)),
         ],
         compiler_params=pltpu.CompilerParams(vmem_limit_bytes=62 * MIB),
     )(gathered)

time: 61.9 us -> 52.7 us (0.85); the launches traced: 60.9 us -> 52.5 us
  Pallas kernels: 60.9 us -> 52.5 us
    pallas_call x1, Pallas kernels: 13.9 us -> 9.09 us  [correlate(): pl.pallas_call(functools.partial(correlate_kernel, inverse), out_shape=ja...]
    pallas_call x1, Pallas kernels: 47 us -> 43.4 us  [spread(): pl.pallas_call(functools.partial(spread_kernel, count, owners), out_shape...]
where the time goes in v4:
time: 52.7 us; the launch traced here: 52.5 us
  Pallas kernels  52.5 us (100%)
    pallas_call x1, Pallas kernels, spread(): pl.pallas_call(functools.partial(spread_kernel, count, owners), out_shape...  43.4 us
    pallas_call x1, Pallas kernels, correlate(): pl.pallas_call(functools.partial(correlate_kernel, inverse), out_shape=ja...  9.09 us

profile of v4, /device:TPU:0, one launch (start us, length us, event | category | flops | bytes accessed | tf_op | source)
XLA Modules:
  0.0 52.5 jit_solution(4519358116281996950)
XLA Ops:
  0.0 43.4 %shard_map.55.gathered = bf16[4,2,8,5,32,128]{5,4,3,2,1,0:T(8,128)(2,1)} custom-call(bf16[2,256,4096]{2,1,0:T(8,128)(2,1)} %voltage.1, f32[4,1024]{1,0:T(4,128)} %constant.4.clone.coeffs, bf16[256,1024]{1,0:T(8,128)(2,1)} %constant.5.clone.table, s32[1,128]{1,0:T(1,128)} %flags.1, s32[1,128]{1,0:T(1,128)} %bitcast.1), custom_call_target="tpu_custom_call" | custom-call | tf_op jit(solution)/shard_map/pallas_call | solution.py:288
  43.5 9.1 %shard_map.56 = bf16[20,2,256,1024]{3,2,1,0:T(8,128)(2,1)} custom-call(bf16[4,2,8,5,32,128]{5,4,3,2,1,0:T(8,128)(2,1)} %shard_map.55.gathered), custom_call_target="tpu_custom_call" | custom-call | tf_op jit(solution)/shard_map/pallas_call | solution.py:364

commit v5 on v4

--- a/solution.py
+++ b/solution.py
@@ -16,7 +16,8 @@
 CAP = 20
 QUAD = 4
 GROUPS = CAP // QUAD
-HALVES = 2
+HALVES = 1
+LOADS = 4
 LAG = 3
 WINDOW = 4
 DEPTH = 2
@@ -41,13 +42,13 @@
 
 
 def spread_kernel(
-    count, owners, voltage, coeffs, table, flags, owner_slot, gathered,
-    samples, slot_table, weighted, halo_out, halo_in, parts, outgoing,
-    load_sem, halo_send, halo_recv, local_sem,
+    count, owners, voltage, coeffs, table_hbm, flags, owner_slot, gathered,
+    samples, table, slot_table, weighted, halo_out, halo_in, parts, outgoing,
+    load_sem, table_sem, halo_send, halo_recv, local_sem,
     a_send, a_recv, x_send, x_recv, y_send, y_recv, d_send, d_recv,
 ):
     feed, me = lax.axis_index("feed"), lax.axis_index("freq")
-    feeds = samples.shape[2]
+    feeds = samples.shape[1] // HALVES
     band = flags.shape[1]
     rows = slot_table.shape[0]
     along_x, along_y = feed ^ 1, feed ^ 2
@@ -59,14 +60,16 @@
     for other in (along_x, along_y):
         pl.semaphore_signal(barrier, inc=1, device_id=(other, me), device_id_type=MESH)
 
-    loads = [
-        pltpu.make_async_copy(
-            voltage.at[:, half * feeds : (half + 1) * feeds, :], samples.at[half], load_sem.at[half]
-        )
-        for half in range(HALVES)
-    ]
-    for load in loads:
-        load.start()
+    tables_in = pltpu.make_async_copy(table_hbm, table, table_sem)
+    tables_in.start()
+    share = samples.shape[1] // LOADS
+
+    def load(index):
+        here = slice(index * share, (index + 1) * share)
+        return pltpu.make_async_copy(voltage.at[:, here, :], samples.at[:, here, :], load_sem.at[index])
+
+    for index in range(LOADS):
+        load(index).start()
 
     row = lax.broadcasted_iota(jnp.int32, (rows, band), 0)
     slot = row // (2 * QUAD) * QUAD + row % QUAD
@@ -75,38 +78,48 @@
     imag_row = row // QUAD % 2 == 1
     real_kept = jnp.where(imag_row, 0.0, kept)
     imag_kept = jnp.where(imag_row, kept, 0.0)
+    tables_in.wait()
     for part, pick in enumerate(([real_kept, -imag_kept], [imag_kept, real_kept])):
         slot_table[:, part * CH : (part + 1) * CH] = jnp.dot(
             jnp.concatenate(pick, 1).astype(jnp.bfloat16), table[...], preferred_element_type=jnp.float32
         ).astype(jnp.bfloat16)
 
-    def weigh(half, sums):
+    sums = [
+        [(tap, spectrum + tap - count) for tap in range(TAPS) if 0 <= spectrum + tap - count < count]
+        for spectrum in range(count - halo, count)
+    ] + [[(tap, spectrum + tap) for tap in range(TAPS) if spectrum + tap < count] for spectrum in range(count)]
+
+    def weigh(half):
         tall = 32
-
-        @pl.loop(0, feeds // tall)
-        def _(index):
-            first = pl.multiple_of(index * tall, tall)
-            for part in range(2):
-                for lane in range(0, CH, 128):
-                    blocks = [
-                        samples[
-                            half, part, pl.ds(first, tall), block * CH + lane : block * CH + lane + 128
-                        ].astype(jnp.float32)
-                        for block in range(count)
-                    ]
-                    for place, pairs in enumerate(sums):
-                        total = None
-                        for tap, block in pairs:
-                            term = blocks[block] * coeffs[tap : tap + 1, lane : lane + 128]
-                            total = term if total is None else total + term
-                        weighted[
-                            pl.ds(place * feeds + first, tall), part * CH + lane : part * CH + lane + 128
-                        ] = total.astype(jnp.bfloat16)
-
-    def transform(places):
+        for index in range(half * LOADS // HALVES, (half + 1) * LOADS // HALVES):
+            load(index).wait()
+
+            @pl.loop(0, share // tall)
+            def _(step):
+                first = pl.multiple_of(index * share + step * tall, tall)
+                placed = first - half * feeds
+                for part in range(2):
+                    for lane in range(0, CH, 128):
+                        blocks = [
+                            samples[
+                                part, pl.ds(first, tall), block * CH + lane : block * CH + lane + 128
+                            ].astype(jnp.float32)
+                            for block in range(count)
+                        ]
+                        for place, pairs in enumerate(sums):
+                            total = None
+                            for tap, block in pairs:
+                                term = blocks[block] * coeffs[tap : tap + 1, lane : lane + 128]
+                                total = term if total is None else total + term
+                            weighted[
+                                pl.ds(pl.multiple_of(place * feeds + placed, tall), tall),
+                                part * CH + lane : part * CH + lane + 128,
+                            ] = total.astype(jnp.bfloat16)
+
+    def transform(start, stop):
         return lax.dot_general(
             slot_table[...],
-            weighted[0 : places * feeds, :],
+            weighted[start * feeds : stop * feeds, :],
             (((1,), (1,)), ((), ())),
             preferred_element_type=jnp.float32,
         )
@@ -122,14 +135,7 @@
         )
 
     def send_halo(half):
-        weigh(
-            half,
-            [
-                [(tap, spectrum + tap - count) for tap in range(TAPS) if 0 <= spectrum + tap - count < count]
-                for spectrum in range(count - halo, count)
-            ],
-        )
-        halo_out[half] = transform(halo).astype(jnp.bfloat16)
+        halo_out[half] = transform(0, halo).astype(jnp.bfloat16)
         if half == 0:
             pl.semaphore_wait(barrier, owners + 1)
 
@@ -137,17 +143,8 @@
         def _():
             backward(half).start()
 
-    def weigh_own(half):
-        weigh(
-            half,
-            [
-                [(tap, spectrum + tap) for tap in range(TAPS) if spectrum + tap < count]
-                for spectrum in range(count)
-            ],
-        )
-
     def transform_own():
-        parts[...] = transform(count)
+        parts[...] = transform(halo, halo + count)
 
     def finish(half):
         @pl.when(me < owners - 1)
@@ -230,25 +227,19 @@
         if len(handled) > DEPTH:
             pass_on(*handled[-1 - DEPTH])
 
-    loads[0].wait()
+    weigh(0)
     send_halo(0)
-    weigh_own(0)
     transform_own()
-    for half in range(1, HALVES):
-        loads[half].wait()
-        send_halo(half)
+    if HALVES > 1:
+        weigh(1)
+        send_halo(1)
     finish(0)
     keep(0).start()
-    if HALVES == 1:
-        handle(steps[0], 0)
-        leave(0, WINDOW)
-    else:
-        handle(early[0], 0)
-        leave(0, WINDOW)
-        weigh_own(1)
-        handle(early[1], 0)
+    handle((0, 0), 0)
+    leave(0, WINDOW)
+    if HALVES > 1:
         transform_own()
-        for step in early[2:]:
+        for step in early[1:]:
             handle(step, 0)
         finish(1)
         keep(1).start()
@@ -290,18 +281,20 @@
         out_shape=jax.ShapeDtypeStruct(
             (feed_groups, HALVES, owners, GROUPS, tall, feeds), jnp.bfloat16
         ),
-        in_specs=[anywhere] + [vmem] * 4,
+        in_specs=[anywhere, vmem, anywhere, vmem, vmem],
         out_specs=anywhere,
         scratch_shapes=[
-            pltpu.VMEM((HALVES, 2, feeds, samples), jnp.bfloat16),
+            pltpu.VMEM((2, HALVES * feeds, samples), jnp.bfloat16),
+            pltpu.VMEM((2 * band, CH), jnp.bfloat16),
             pltpu.VMEM((rows, 2 * CH), jnp.bfloat16),
-            pltpu.VMEM((count * feeds, 2 * CH), jnp.bfloat16),
+            pltpu.VMEM(((count + TAPS - 1) * feeds, 2 * CH), jnp.bfloat16),
             pltpu.VMEM((HALVES, rows, (TAPS - 1) * feeds), jnp.bfloat16),
             pltpu.VMEM((HALVES, rows, (TAPS - 1) * feeds), jnp.bfloat16),
             pltpu.VMEM((rows, count * feeds), jnp.float32),
             pltpu.VMEM((HALVES, owners * GROUPS, tall, feeds), jnp.bfloat16),
         ]
-        + [dma((HALVES,))] * 4
+        + [dma((LOADS,)), dma]
+        + [dma((HALVES,))] * 3
         + [dma((HALVES, owners))] * 8,
         compiler_params=pltpu.CompilerParams(
             collective_id=0, has_side_effects=True, vmem_limit_bytes=62 * MIB
@@ -319,8 +312,7 @@
     def store(slot, part):
         return pltpu.make_async_copy(results.at[slot, part], out.at[slot, part], out_sem.at[slot, part])
 
-    for group in range(GROUPS):
-        fetch(group).start()
+    fetch(0).start()
     source = lax.broadcasted_iota(jnp.int32, (depth, depth), 0)
     target = lax.broadcasted_iota(jnp.int32, (depth, depth), 1)
     imag = target // QUAD % 2
@@ -329,10 +321,16 @@
     ).astype(jnp.bfloat16)
     lane = lax.broadcasted_iota(jnp.int32, (1, depth), 1)
     mine = lax.axis_index("feed")
+    fetch(0).wait()
+    for group in range(1, GROUPS):
+        fetch(group).start()
 
     @pl.loop(0, GROUPS)
     def _(group):
-        fetch(group).wait()
+        @pl.when(group > 0)
+        def _():
+            fetch(group).wait()
+
         own = jnp.concatenate([held[group, mine, half].reshape(depth, some).T for half in range(halves)], 0)
         bases[0] = own
         bases[1] = jnp.dot(own, turn[...], preferred_element_type=jnp.float32).astype(jnp.bfloat16)

time: 52.7 us -> 56.5 us (1.072)
  Pallas kernels: 52.5 us -> 56.2 us
    pallas_call x1, Pallas kernels: 43.4 us -> 47.1 us  [spread(): pl.pallas_call(functools.partial(spread_kernel, count, owners), out_shape...]
where the time goes in v5:
time: 56.5 us; the launch traced here: 56.3 us
  Pallas kernels  56.2 us (99%)
    pallas_call x1, Pallas kernels, spread(): pl.pallas_call(functools.partial(spread_kernel, count, owners), out_shape...  47.1 us
    pallas_call x1, Pallas kernels, correlate(): pl.pallas_call(functools.partial(correlate_kernel, inverse), out_shape=ja...  9.1 us

profile of v5, /device:TPU:0, one launch (start us, length us, event | category | flops | bytes accessed | tf_op | source)
XLA Modules:
  0.0 56.3 jit_solution(9963732906045971912)
XLA Ops:
  0.0 47.1 %shard_map.55.gathered = bf16[4,1,8,5,32,256]{5,4,3,2,1,0:T(8,128)(2,1)} custom-call(bf16[2,256,4096]{2,1,0:T(8,128)(2,1)} %voltage.1, f32[4,1024]{1,0:T(4,128)} %constant.4.clone.coeffs, bf16[256,1024]{1,0:T(8,128)(2,1)} %constant.5.clone.table_hbm, s32[1,128]{1,0:T(1,128)} %flags.1, s32[1,128]{1,0:T(1,128)} %bitcast.1), custom_call_target="tpu_custom_call" | custom-call | tf_op jit(solution)/shard_map/pallas_call | solution.py:279
  47.2 9.1 %shard_map.56 = bf16[20,2,256,1024]{3,2,1,0:T(8,128)(2,1)} custom-call(bf16[4,1,8,5,32,256]{5,4,3,2,1,0:T(8,128)(2,1)} %shard_map.55.gathered), custom_call_target="tpu_custom_call" | custom-call | tf_op jit(solution)/shard_map/pallas_call | solution.py:362

commit v6 on v5

--- a/solution.py
+++ b/solution.py
@@ -16,11 +16,11 @@
 CAP = 20
 QUAD = 4
 GROUPS = CAP // QUAD
-HALVES = 1
+HALVES = 2
 LOADS = 4
 LAG = 3
-WINDOW = 4
-DEPTH = 2
+WINDOW = 1024
+DEPTH = 3
 MESH = pl.DeviceIdType.MESH
 MIB = 1024 * 1024
 

time: 56.5 us -> 53.3 us (0.943)
  Pallas kernels: 56.2 us -> 52.8 us
    pallas_call x1, Pallas kernels: 47.1 us -> 43.7 us  [spread(): pl.pallas_call(functools.partial(spread_kernel, count, owners), out_shape...]
where the time goes in v6:
time: 53.3 us; the launch traced here: 52.8 us
  Pallas kernels  52.8 us (99%)
    pallas_call x1, Pallas kernels, spread(): pl.pallas_call(functools.partial(spread_kernel, count, owners), out_shape...  43.7 us
    pallas_call x1, Pallas kernels, correlate(): pl.pallas_call(functools.partial(correlate_kernel, inverse), out_shape=ja...  9.09 us

profile of v6, /device:TPU:0, one launch (start us, length us, event | category | flops | bytes accessed | tf_op | source)
XLA Modules:
  0.0 52.8 jit_solution(979299431848491982)
XLA Ops:
  0.0 43.7 %shard_map.55.gathered = bf16[4,2,8,5,32,128]{5,4,3,2,1,0:T(8,128)(2,1)} custom-call(bf16[2,256,4096]{2,1,0:T(8,128)(2,1)} %voltage.1, f32[4,1024]{1,0:T(4,128)} %constant.4.clone.coeffs, bf16[256,1024]{1,0:T(8,128)(2,1)} %constant.5.clone.table_hbm, s32[1,128]{1,0:T(1,128)} %flags.1, s32[1,128]{1,0:T(1,128)} %bitcast.1), custom_call_target="tpu_custom_call" | custom-call | tf_op jit(solution)/shard_map/pallas_call | solution.py:279
  43.7 9.1 %shard_map.56 = bf16[20,2,256,1024]{3,2,1,0:T(8,128)(2,1)} custom-call(bf16[4,2,8,5,32,128]{5,4,3,2,1,0:T(8,128)(2,1)} %shard_map.55.gathered), custom_call_target="tpu_custom_call" | custom-call | tf_op jit(solution)/shard_map/pallas_call | solution.py:362

commit v7 on v6

--- a/solution.py
+++ b/solution.py
@@ -19,8 +19,8 @@
 HALVES = 2
 LOADS = 4
 LAG = 3
-WINDOW = 1024
-DEPTH = 3
+WINDOW = 6
+DEPTH = 2
 MESH = pl.DeviceIdType.MESH
 MIB = 1024 * 1024
 
@@ -84,15 +84,17 @@
             jnp.concatenate(pick, 1).astype(jnp.bfloat16), table[...], preferred_element_type=jnp.float32
         ).astype(jnp.bfloat16)
 
-    sums = [
+    ahead = [
         [(tap, spectrum + tap - count) for tap in range(TAPS) if 0 <= spectrum + tap - count < count]
         for spectrum in range(count - halo, count)
-    ] + [[(tap, spectrum + tap) for tap in range(TAPS) if spectrum + tap < count] for spectrum in range(count)]
-
-    def weigh(half):
+    ]
+    within = [[(tap, spectrum + tap) for tap in range(TAPS) if spectrum + tap < count] for spectrum in range(count)]
+
+    def weigh(half, sums):
         tall = 32
         for index in range(half * LOADS // HALVES, (half + 1) * LOADS // HALVES):
-            load(index).wait()
+            if sums is ahead:
+                load(index).wait()
 
             @pl.loop(0, share // tall)
             def _(step):
@@ -116,10 +118,10 @@
                                 part * CH + lane : part * CH + lane + 128,
                             ] = total.astype(jnp.bfloat16)
 
-    def transform(start, stop):
+    def transform(places):
         return lax.dot_general(
             slot_table[...],
-            weighted[start * feeds : stop * feeds, :],
+            weighted[0 : places * feeds, :],
             (((1,), (1,)), ((), ())),
             preferred_element_type=jnp.float32,
         )
@@ -135,7 +137,7 @@
         )
 
     def send_halo(half):
-        halo_out[half] = transform(0, halo).astype(jnp.bfloat16)
+        halo_out[half] = transform(halo).astype(jnp.bfloat16)
         if half == 0:
             pl.semaphore_wait(barrier, owners + 1)
 
@@ -144,7 +146,7 @@
             backward(half).start()
 
     def transform_own():
-        parts[...] = transform(halo, halo + count)
+        parts[...] = transform(count)
 
     def finish(half):
         @pl.when(me < owners - 1)
@@ -227,19 +229,22 @@
         if len(handled) > DEPTH:
             pass_on(*handled[-1 - DEPTH])
 
-    weigh(0)
+    weigh(0, ahead)
     send_halo(0)
+    weigh(0, within)
     transform_own()
     if HALVES > 1:
-        weigh(1)
+        weigh(1, ahead)
         send_halo(1)
     finish(0)
     keep(0).start()
     handle((0, 0), 0)
     leave(0, WINDOW)
     if HALVES > 1:
+        weigh(1, within)
+        handle(early[1], 0)
         transform_own()
-        for step in early[1:]:
+        for step in early[2:]:
             handle(step, 0)
         finish(1)
         keep(1).start()
@@ -287,7 +292,7 @@
             pltpu.VMEM((2, HALVES * feeds, samples), jnp.bfloat16),
             pltpu.VMEM((2 * band, CH), jnp.bfloat16),
             pltpu.VMEM((rows, 2 * CH), jnp.bfloat16),
-            pltpu.VMEM(((count + TAPS - 1) * feeds, 2 * CH), jnp.bfloat16),
+            pltpu.VMEM((count * feeds, 2 * CH), jnp.bfloat16),
             pltpu.VMEM((HALVES, rows, (TAPS - 1) * feeds), jnp.bfloat16),
             pltpu.VMEM((HALVES, rows, (TAPS - 1) * feeds), jnp.bfloat16),
             pltpu.VMEM((rows, count * feeds), jnp.float32),

time: 53.3 us -> 52.8 us (level)
  no operation moved by 1% of the time
where the time goes in v7:
time: 52.8 us; the launch traced here: 52.6 us
  Pallas kernels  52.6 us (100%)
    pallas_call x1, Pallas kernels, spread(): pl.pallas_call(functools.partial(spread_kernel, count, owners), out_shape...  43.5 us
    pallas_call x1, Pallas kernels, correlate(): pl.pallas_call(functools.partial(correlate_kernel, inverse), out_shape=ja...  9.1 us

profile of v7, /device:TPU:0, one launch (start us, length us, event | category | flops | bytes accessed | tf_op | source)
XLA Modules:
  0.0 52.6 jit_solution(8038453889021240240)
XLA Ops:
  0.0 43.5 %shard_map.55.gathered = bf16[4,2,8,5,32,128]{5,4,3,2,1,0:T(8,128)(2,1)} custom-call(bf16[2,256,4096]{2,1,0:T(8,128)(2,1)} %voltage.1, f32[4,1024]{1,0:T(4,128)} %constant.4.clone.coeffs, bf16[256,1024]{1,0:T(8,128)(2,1)} %constant.5.clone.table_hbm, s32[1,128]{1,0:T(1,128)} %flags.1, s32[1,128]{1,0:T(1,128)} %bitcast.1), custom_call_target="tpu_custom_call" | custom-call | tf_op jit(solution)/shard_map/pallas_call | solution.py:284
  43.5 9.1 %shard_map.56 = bf16[20,2,256,1024]{3,2,1,0:T(8,128)(2,1)} custom-call(bf16[4,2,8,5,32,128]{5,4,3,2,1,0:T(8,128)(2,1)} %shard_map.55.gathered), custom_call_target="tpu_custom_call" | custom-call | tf_op jit(solution)/shard_map/pallas_call | solution.py:367
